TPU v7x, 32 devices: a whole 2x2x4 slice. The times are simulated.
32 devices in a mesh: chan: 4 (over y, x), bl: 8 (over z, core).
Axes of the slice: x: 2, y: 2, z: 4, core: 2. Of those that a mesh axis runs over, the one named last changes fastest.
Arguments:
- grid: float32 [64, 128, 256], P('bl'), may hold values from -6 to 6
- tile_list: int32 [4, 512], P('chan', 'bl'), may hold values from 0 to 63, as said below
- owner_map: int32 [64], replicated, may hold values from 0 to 63, as said below
- offsets: int32 [4, 512, 2], P('chan', 'bl'), may hold values from 4 to 60
- positions: float32 [4, 512, 2, 128], P('chan', 'bl'), may hold values from 0 to 64
- observed: float32 [4, 512, 2, 128], P('chan', 'bl'), may hold values from -6 to 6
- weights: float32 [4, 512, 128], P('chan', 'bl'), may hold values from 0.1 to 1
Outputs:
- new_grid: float32 [64, 128, 256], P('bl', 'chan')
- residual: float32 [4, 512, 2, 128], P('chan', 'bl')
Inputs may be any that keep to these rules, and one draw needn't show every extreme that they name: A permutation: tile t lies on index owner_map[t] // 8 of bl, at place owner_map[t] % 8 there. `tile_list`: of the 64 blocks held by one device (one channel group, one index of bl), at most 16 name tiles of any one owner; in every channel group some owner receives exactly 16 blocks from every device of that group.
All inputs are finite; a program needn't handle non-finite values.
Results may differ from a plain program's by a relative error of at most 0.008.
Values sent between devices are 32-bit elements; how exact they have to be, the bound alone decides.
A program may use at most 128 MiB of HBM per device.

v0:
```python
import math

import jax
import jax.numpy as jnp
from jax import lax
from jax.sharding import PartitionSpec as P

kernel_beta = 18.4
half_support = 4.0
step_length = 1.0
ridge_weight = 0.5


def spheroid(offset):
    scaled = offset / half_support
    inside = scaled * scaled < 1.0
    root_term = jnp.sqrt(jnp.maximum(1.0 - scaled * scaled, 0.0))
    return jnp.where(inside, jnp.exp(kernel_beta * (root_term - 1.0)), 0.0)


def shards(grid, tile_list, owner_map, offsets, positions, observed, weights):
    owners = lax.axis_size("bl")
    tile_dev = grid.shape[0]
    tile_width = grid.shape[1]
    block_count = tile_list.shape[1]
    capacity = 2 * block_count // owners
    slots_all = owners * capacity
    tile_ids = tile_list[0]
    tile_table = jnp.arange(owner_map.shape[0], dtype=jnp.int32)
    slot_index = jnp.sum(
        jnp.where(tile_ids[:, None] == tile_table[None, :], owner_map[None, :], 0), axis=1
    )
    owner_index = slot_index // tile_dev
    local_slot = slot_index % tile_dev
    owner_onehot = (owner_index[:, None] == jnp.arange(owners, dtype=jnp.int32)[None, :]).astype(
        jnp.int32
    )
    earlier_count = jnp.cumsum(owner_onehot, axis=0) - owner_onehot
    place_rank = jnp.sum(owner_onehot * earlier_count, axis=1)
    send_slot = owner_index * capacity + place_rank
    coords = offsets[0].astype(jnp.float32)[..., None] + positions[0]
    payload = jnp.concatenate([observed[0], weights[0][:, None, :], coords], axis=1)
    outgoing = jnp.zeros((slots_all,) + payload.shape[1:], jnp.float32).at[send_slot].set(payload)
    slot_labels = (
        jnp.zeros((slots_all,), jnp.float32).at[send_slot].set(local_slot.astype(jnp.float32))
    )
    incoming, in_labels = (
        lax.all_to_all(outgoing, "bl", split_axis=0, concat_axis=0, tiled=True),
        lax.all_to_all(slot_labels, "bl", split_axis=0, concat_axis=0, tiled=True),
    )
    grid_low = grid.astype(jnp.bfloat16)
    group_size = math.gcd(slots_all, 16)
    cell_index = jnp.arange(tile_width, dtype=jnp.float32)
    tile_places = jnp.arange(tile_dev, dtype=jnp.int32)

    def degrid(batch_data, tile_index):
        tiles_now = grid_low[tile_index]
        observed_now = batch_data[:, 0:2]
        weight_now = batch_data[:, 2]
        u_coord = batch_data[:, 3]
        v_coord = batch_data[:, 4]
        kernel_u = spheroid(cell_index[None, None, :] - u_coord[:, :, None]).astype(jnp.bfloat16)
        kernel_v = spheroid(cell_index[None, None, :] - v_coord[:, :, None]).astype(jnp.bfloat16)
        projected = jnp.einsum(
            "gju,guw->gjw", kernel_u, tiles_now, preferred_element_type=jnp.float32
        )
        kernel_wide = kernel_v.astype(jnp.float32)
        model_real = jnp.sum(projected[:, :, :tile_width] * kernel_wide, axis=2)
        model_imag = jnp.sum(projected[:, :, tile_width:] * kernel_wide, axis=2)
        residual_now = weight_now[:, None, :] * (
            jnp.stack([model_real, model_imag], axis=1) - observed_now
        )
        spread = jnp.concatenate(
            [residual_now[:, 0, :, None] * kernel_wide, residual_now[:, 1, :, None] * kernel_wide],
            axis=2,
        ).astype(jnp.bfloat16)
        return (residual_now, kernel_u, spread)

    batches = incoming.reshape(
        slots_all // group_size, group_size, incoming.shape[1], incoming.shape[2]
    )
    batch_labels = in_labels.reshape(slots_all // group_size, group_size).astype(jnp.int32)
    share_rows = tile_width // lax.axis_size("chan")
    share_start = lax.axis_index("chan") * share_rows

    def process(gradient, block_item):
        batch_data, tile_index = block_item
        residual_now, kernel_u, spread = degrid(batch_data, tile_index)
        contrib = jnp.einsum("gju,gjw->guw", kernel_u, spread, preferred_element_type=jnp.float32)
        selector = (tile_index[:, None] == tile_places[None, :]).astype(jnp.float32)
        gradient = gradient + jnp.einsum(
            "gt,guw->tuw", selector, contrib, precision=lax.Precision.HIGHEST
        )
        return (gradient, residual_now)

    gradient, residual_all = lax.scan(
        process, jnp.zeros(grid.shape, jnp.float32), (batches, batch_labels)
    )
    grad_share = lax.psum_scatter(gradient, "chan", scatter_dimension=1, tiled=True)
    residual_all = residual_all.reshape(slots_all, 2, residual_all.shape[-1])
    returned = lax.all_to_all(residual_all, "bl", split_axis=0, concat_axis=0, tiled=True)
    my_residual = returned[send_slot][None]
    own_rows = lax.dynamic_slice_in_dim(grid, share_start, share_rows, 1)
    new_grid = own_rows - step_length * (grad_share + ridge_weight * own_rows)
    return (new_grid, my_residual)


def solution(mesh):
    in_specs = (
        P("bl", None, None),
        P("chan", "bl"),
        P(),
        P("chan", "bl", None),
        P("chan", "bl", None, None),
        P("chan", "bl", None, None),
        P("chan", "bl", None),
    )
    out_specs = (P("bl", "chan", None), P("chan", "bl", None, None))
    return jax.shard_map(shards, mesh=mesh, in_specs=in_specs, out_specs=out_specs, check_vma=False)
```

profile of v0, /device:TPU:0, one launch (start us, length us, event | category | flops | bytes accessed | tf_op | source)
XLA Modules:
  0.0 159.7 jit_solution(3961261230285422628)
XLA Ops:
  10.0 6.3 %all-to-all-start = ((f32[8,16,1]{1,2,0:T(1,128)}), f32[8,16,1]{1,2,0:T(1,128)S(1)}, u32[]{:S(2)}, u32[]{:S(2)}) async-start(f32[8,16,1]{1,2,0:T(1,128)} %bitcast.4), calls=%async_computation | async-start | bytes 8192 | tf_op jit(solution)/shard_map/all_to_all | solution.py:49
  19.9 6.5 %scatter_fusion = f32[128,5,128]{2,1,0:T(8,128)} fusion(f32[128,5,128]{2,1,0:T(8,128)} %broadcast_in_dim.56, s32[64]{0:T(128)S(1)} %fusion.61, f32[64,5,128]{2,1,0:T(8,128)S(1)} %pad_maximum_fusion), kind=kCustom, calls=%fused_computation.3 | custom fusion | bytes 491776 | tf_op jit(solution)/shard_map/scatter | solution.py:43
  26.3 5.1 %all-to-all-start.1 = ((f32[128,5,128]{2,1,0:T(8,128)}), f32[128,5,128]{2,1,0:T(8,128)S(1)}, u32[]{:S(2)}, u32[]{:S(2)}) async-start(f32[128,5,128]{2,1,0:T(8,128)} %scatter_fusion), calls=%async_computation.1 | async-start | bytes 1048576 | tf_op jit(solution)/shard_map/all_to_all | solution.py:48
  31.5 15.2 %all-to-all-done.1 = f32[128,5,128]{2,1,0:T(8,128)S(1)} async-done(((f32[128,5,128]{2,1,0:T(8,128)}), f32[128,5,128]{2,1,0:T(8,128)S(1)}, u32[]{:S(2)}, u32[]{:S(2)}) %all-to-all-start.1) | async-done | bytes 327712 | tf_op jit(solution)/shard_map/all_to_all | solution.py:48
  46.8 74.7 %while.17 = (s32[]{:T(128)}, f32[8,128,256]{2,0,1:T(8,128)}, f32[8,16,2,128]{3,1,0,2:T(8,128)S(1)}, s32[8,16]{1,0:T(8,128)S(1)}, f32[8,16,5,128]{3,1,2,0:T(8,128...) while((s32[]{:T(128)}, f32[8,128,256]{2,0,1:T(8,128)}, ...), condition=%wide.region_8.9_spmd.clone.clone, body=%wide.region_5.8_spmd.clone.clone.sunk | while | flops 334505152 | bytes 16036399 | solution.py:96
  48.6 1.2 fusion.87
  50.8 1.3 fusion.89
  52.1 3.0 %fusion.91 = f32[8,128,256]{2,0,1:T(8,128)} fusion(f32[16,128,256]{2,1,0:T(8,128)S(1)} %fusion.89, f32[8,128,256]{2,0,1:T(8,128)} %get-tuple-element.295, pred[]{:T(512)S(6)} %compare.18, s32[16]{0:T(128)S(1)} %fusion.90), kind=kOutput, calls=%fused_computation.14.clone.1 | convolution fusion | flops 50856064 | bytes 4194369 | tf_op jit(solution)/shard_map/while/body/eval_jaxpr/gt,guw->tuw/dot_general | solution.py:91
  56.9 1.2 fusion.87
  59.1 1.3 fusion.89
  60.4 4.2 %fusion.91 = f32[8,128,256]{2,0,1:T(8,128)} fusion(f32[16,128,256]{2,1,0:T(8,128)S(1)} %fusion.89, f32[8,128,256]{2,0,1:T(8,128)} %get-tuple-element.295, pred[]{:T(512)S(6)} %compare.18, s32[16]{0:T(128)S(1)} %fusion.90), kind=kOutput, calls=%fused_computation.14.clone.1 | convolution fusion | flops 50856064 | bytes 4194369 | tf_op jit(solution)/shard_map/while/body/eval_jaxpr/gt,guw->tuw/dot_general | solution.py:91
  66.4 1.2 fusion.87
  68.6 1.3 fusion.89
  69.9 4.2 %fusion.91 = f32[8,128,256]{2,0,1:T(8,128)} fusion(f32[16,128,256]{2,1,0:T(8,128)S(1)} %fusion.89, f32[8,128,256]{2,0,1:T(8,128)} %get-tuple-element.295, pred[]{:T(512)S(6)} %compare.18, s32[16]{0:T(128)S(1)} %fusion.90), kind=kOutput, calls=%fused_computation.14.clone.1 | convolution fusion | flops 50856064 | bytes 4194369 | tf_op jit(solution)/shard_map/while/body/eval_jaxpr/gt,guw->tuw/dot_general | solution.py:91
  75.9 1.2 fusion.87
  78.1 1.3 fusion.89
  79.4 4.2 %fusion.91 = f32[8,128,256]{2,0,1:T(8,128)} fusion(f32[16,128,256]{2,1,0:T(8,128)S(1)} %fusion.89, f32[8,128,256]{2,0,1:T(8,128)} %get-tuple-element.295, pred[]{:T(512)S(6)} %compare.18, s32[16]{0:T(128)S(1)} %fusion.90), kind=kOutput, calls=%fused_computation.14.clone.1 | convolution fusion | flops 50856064 | bytes 4194369 | tf_op jit(solution)/shard_map/while/body/eval_jaxpr/gt,guw->tuw/dot_general | solution.py:91
  85.4 1.2 fusion.87
  87.6 1.3 fusion.89
  88.9 4.2 %fusion.91 = f32[8,128,256]{2,0,1:T(8,128)} fusion(f32[16,128,256]{2,1,0:T(8,128)S(1)} %fusion.89, f32[8,128,256]{2,0,1:T(8,128)} %get-tuple-element.295, pred[]{:T(512)S(6)} %compare.18, s32[16]{0:T(128)S(1)} %fusion.90), kind=kOutput, calls=%fused_computation.14.clone.1 | convolution fusion | flops 50856064 | bytes 4194369 | tf_op jit(solution)/shard_map/while/body/eval_jaxpr/gt,guw->tuw/dot_general | solution.py:91
  97.1 1.3 fusion.89
  98.4 4.2 %fusion.91 = f32[8,128,256]{2,0,1:T(8,128)} fusion(f32[16,128,256]{2,1,0:T(8,128)S(1)} %fusion.89, f32[8,128,256]{2,0,1:T(8,128)} %get-tuple-element.295, pred[]{:T(512)S(6)} %compare.18, s32[16]{0:T(128)S(1)} %fusion.90), kind=kOutput, calls=%fused_computation.14.clone.1 | convolution fusion | flops 50856064 | bytes 4194369 | tf_op jit(solution)/shard_map/while/body/eval_jaxpr/gt,guw->tuw/dot_general | solution.py:91
  106.6 1.3 fusion.89
  107.9 4.2 %fusion.91 = f32[8,128,256]{2,0,1:T(8,128)} fusion(f32[16,128,256]{2,1,0:T(8,128)S(1)} %fusion.89, f32[8,128,256]{2,0,1:T(8,128)} %get-tuple-element.295, pred[]{:T(512)S(6)} %compare.18, s32[16]{0:T(128)S(1)} %fusion.90), kind=kOutput, calls=%fused_computation.14.clone.1 | convolution fusion | flops 50856064 | bytes 4194369 | tf_op jit(solution)/shard_map/while/body/eval_jaxpr/gt,guw->tuw/dot_general | solution.py:91
  116.1 1.3 fusion.89
  117.3 4.2 %fusion.91 = f32[8,128,256]{2,0,1:T(8,128)} fusion(f32[16,128,256]{2,1,0:T(8,128)S(1)} %fusion.89, f32[8,128,256]{2,0,1:T(8,128)} %get-tuple-element.295, pred[]{:T(512)S(6)} %compare.18, s32[16]{0:T(128)S(1)} %fusion.90), kind=kOutput, calls=%fused_computation.14.clone.1 | convolution fusion | flops 50856064 | bytes 4194369 | tf_op jit(solution)/shard_map/while/body/eval_jaxpr/gt,guw->tuw/dot_general | solution.py:91
  121.6 2.6 %copy.46 = f32[8,128,256]{2,1,0:T(8,128)} copy(f32[8,128,256]{2,0,1:T(8,128)} %get-tuple-element.129) | data formatting | bytes 2097152 | tf_op jit(solution)/shard_map/while | solution.py:96
  125.0 3.4 %all-to-all-start.2 = ((f32[128,2,128]{2,1,0:T(2,128)}), f32[128,2,128]{2,1,0:T(2,128)S(1)}, u32[]{:S(2)}, u32[]{:S(2)}) async-start(f32[128,2,128]{2,1,0:T(2,128)} %copy.48), calls=%async_computation.3 | async-start | bytes 262144 | tf_op jit(solution)/shard_map/all_to_all | solution.py:101
  128.4 6.7 %all-to-all-done.2 = f32[128,2,128]{2,1,0:T(2,128)S(1)} async-done(((f32[128,2,128]{2,1,0:T(2,128)}), f32[128,2,128]{2,1,0:T(2,128)S(1)}, u32[]{:S(2)}, u32[]{:S(2)}) %all-to-all-start.2) | async-done | bytes 131104 | tf_op jit(solution)/shard_map/all_to_all | solution.py:101
  135.0 1.3 gather_fusion.1
  136.3 14.7 %reduce-scatter.2.cloned.1.call-done = f32[8,32,256]{2,1,0:T(8,128)} async-done(((f32[8,128,256]{2,1,0:T(8,128)}), f32[8,32,256]{2,1,0:T(8,128)}) %reduce-scatter.2.cloned.1.call-update) | async-done | bytes 262160 | tf_op jit(solution)/shard_map/reduce_scatter | solution.py:99
  151.0 1.8 %add_subtract_fusion = f32[8,32,256]{2,1,0:T(8,128)} fusion(f32[8,32,256]{2,1,0:T(8,128)} %reduce-scatter.2.cloned.1.call-done, f32[8,128,256]{2,1,0:T(8,128)} %param.9, s32[]{:T(128)S(6)} %select_n.72), kind=kLoop, calls=%fused_computation.75 | loop fusion | flops 196608 | bytes 786436 | tf_op jit(solution)/shard_map/sub | solution.py:104
  (108 shorter events, 32.8 us)
Async XLA Ops:
  7.2 24.3 %copy-start = (f32[8,128,256]{2,1,0:T(8,128)S(1)}, f32[8,128,256]{2,1,0:T(8,128)}, u32[]{:S(2)}) copy-start(f32[8,128,256]{2,1,0:T(8,128)} %param.9) | copy-start | bytes 3145732
  10.0 16.3 %all-to-all-start = ((f32[8,16,1]{1,2,0:T(1,128)}), f32[8,16,1]{1,2,0:T(1,128)S(1)}, u32[]{:S(2)}, u32[]{:S(2)}) async-start(f32[8,16,1]{1,2,0:T(1,128)} %bitcast.4), calls=%async_computation | async-start | bytes 8192 | tf_op jit(solution)/shard_map/all_to_all | solution.py:49
  26.3 20.4 %all-to-all-start.1 = ((f32[128,5,128]{2,1,0:T(8,128)}), f32[128,5,128]{2,1,0:T(8,128)S(1)}, u32[]{:S(2)}, u32[]{:S(2)}) async-start(f32[128,5,128]{2,1,0:T(8,128)} %scatter_fusion), calls=%async_computation.1 | async-start | bytes 1048576 | tf_op jit(solution)/shard_map/all_to_all | solution.py:48
  31.4 119.6 %reduce-scatter.2.cloned.1.call-start = ((), (), s32[]{:S(2)}) async-start(), calls=%async_computation.4 | async-start | bytes 1310720 | tf_op jit(solution)/shard_map/reduce_scatter | solution.py:99
  125.0 10.1 %all-to-all-start.2 = ((f32[128,2,128]{2,1,0:T(2,128)}), f32[128,2,128]{2,1,0:T(2,128)S(1)}, u32[]{:S(2)}, u32[]{:S(2)}) async-start(f32[128,2,128]{2,1,0:T(2,128)} %copy.48), calls=%async_computation.3 | async-start | bytes 262144 | tf_op jit(solution)/shard_map/all_to_all | solution.py:101
Sparse Core Ops, SparseCore 0:
  124.3 26.6 reduce-scatter.1
where the time goes:
time: 161 us; the launch traced here: 160 us
  matrix products  51.3 us (32%)
  waiting for transfers between devices  36.6 us (23%)
  other arithmetic  23.4 us (15%)
  local copies, waits for them, and re-layouts  18.7 us (12%)
  starting transfers between devices  14.8 us (9%)
  between operations  14.1 us (9%)
    dot_general x8, matrix products, process(): jnp.einsum('gt,guw->tuw', selector, contrib, precision=lax.Precision.HIGH...  32.6 us
    all_to_all x1, waiting for transfers between devices, shards(): lax.all_to_all(outgoing, 'bl', split_axis=0, concat_axis=0, tiled=True)  15.2 us
    reduce_scatter x1, waiting for transfers between devices, shards(): lax.psum_scatter(gradient, 'chan', scatter_dimension=1, tiled=True)  14.7 us
    dot_general x8, matrix products, process(): jnp.einsum('gju,gjw->guw', kernel_u, spread, preferred_element_type=jnp.f...  10 us
    reduce_sum x8, other arithmetic, degrid(): model_real = jnp.sum(projected[:, :, :tile_width] * kernel_wide, axis=2)  9.41 us
    dot_general x8, matrix products, degrid(): jnp.einsum('gju,guw->gjw', kernel_u, tiles_now, preferred_element_type=jn...  8.65 us
    another operation x8, other arithmetic  8.07 us
    all_to_all x1, waiting for transfers between devices, shards(): lax.all_to_all(residual_all, 'bl', split_axis=0, concat_axis=0, tiled=True)  6.69 us
  transfers between devices with their start and end apart: 4, of which 3 were waited for; matrix products, arithmetic and copies ran while one was open for 8% of the time, Pallas kernels for 0%

commit v1 on v0

v1 whole, which is shorter than its diff:
```python
import functools
import math

import jax
import jax.numpy as jnp
from jax import lax
from jax.experimental import pallas as pl
from jax.experimental.pallas import tpu as pltpu
from jax.sharding import PartitionSpec as P

kernel_beta = 18.4
half_support = 4.0
step_length = 1.0
ridge_weight = 0.5
exponent_scale = kernel_beta / math.log(2.0)
MESH = pl.DeviceIdType.MESH
VMEM = pl.BlockSpec(memory_space=pltpu.VMEM)
SMEM = pl.BlockSpec(memory_space=pltpu.SMEM)
ANY = pl.BlockSpec(memory_space=pl.ANY)


def params(**kw):
    return pltpu.CompilerParams(vmem_limit_bytes=24 * 2**20, **kw)


def label_row(cap):
    return -(-5 * cap // 8) * 8


def pack_kernel(cap, tile_dev, tiles, owners, offs, pos, obs, wts, out, place, count):
    blocks = wts.shape[0]
    lab_row = label_row(cap)
    out[...] = jnp.zeros_like(out)
    for o in range(out.shape[0]):
        count[o] = 0
    lane = lax.broadcasted_iota(jnp.int32, (1, out.shape[2]), 1)

    def body(b, carry):
        slot = owners[tiles[0, b]]
        o = lax.div(slot, tile_dev)
        local = lax.rem(slot, tile_dev).astype(jnp.float32)
        r = count[o]
        count[o] = r + 1
        place[b] = o * (2 * cap) + r
        out[o, pl.ds(r, 1), :] = obs[pl.ds(2 * b, 1), :]
        out[o, pl.ds(r + cap, 1), :] = obs[pl.ds(2 * b + 1, 1), :]
        out[o, pl.ds(r + 2 * cap, 1), :] = wts[pl.ds(b, 1), :]
        u_shift = offs[2 * b].astype(jnp.float32)
        v_shift = offs[2 * b + 1].astype(jnp.float32)
        out[o, pl.ds(r + 3 * cap, 1), :] = u_shift + pos[pl.ds(2 * b, 1), :]
        out[o, pl.ds(r + 4 * cap, 1), :] = v_shift + pos[pl.ds(2 * b + 1, 1), :]
        old = out[o, pl.ds(lab_row, 1), :]
        out[o, pl.ds(lab_row, 1), :] = jnp.where(lane == r, local, old)
        return carry

    lax.fori_loop(0, blocks, body, 0, unroll=4)


def exchange_kernel(n, out, grid, came, tiles_t, send_sem, recv_sem, own_sem):
    me = lax.axis_index("bl")
    barrier = pltpu.get_barrier_semaphore()
    for d in range(1, n):
        pl.semaphore_signal(barrier, inc=1, device_id={"bl": lax.rem(me + d, n)}, device_id_type=MESH)
    pl.semaphore_wait(barrier, n - 1)
    copies = []
    for d in range(1, n):
        peer = lax.rem(me + d, n)
        copy = pltpu.make_async_remote_copy(
            src_ref=out.at[peer],
            dst_ref=came.at[me],
            send_sem=send_sem.at[d],
            recv_sem=recv_sem.at[d],
            device_id={"bl": peer},
            device_id_type=MESH,
        )
        copy.start()
        copies.append(copy)
    own = pltpu.make_async_copy(out.at[me], came.at[me], own_sem)
    own.start()
    for t in range(grid.shape[0]):
        tiles_t[t] = grid[t].T.astype(jnp.bfloat16)
    own.wait()
    for copy in copies:
        copy.wait()


def spheroid(cells, coord):
    d = cells - coord * (1.0 / half_support)
    y = 1.0 - d * d
    ym = jnp.maximum(y, 1e-30)
    z = ym * lax.rsqrt(ym) * exponent_scale - exponent_scale
    return jnp.where(y > 0.0, jnp.exp2(z), 0.0)


def compute_kernel(cap, group, labels, came, tiles_t, gradient, residual):
    width = tiles_t.shape[2]
    vis = came.shape[2]
    gradient[...] = jnp.zeros_like(gradient)
    per = cap // group

    def body(i, carry):
        s = lax.div(i, per)
        k0 = lax.rem(i, per) * group
        cells = lax.broadcasted_iota(jnp.int32, (width, vis), 0).astype(jnp.float32) * (
            1.0 / half_support
        )
        contribs = []
        for g in range(group):
            k = k0 + g
            label = labels[s * cap + k]
            rows = [came[s, pl.ds(k + c * cap, 1), :] for c in range(5)]
            ku = spheroid(cells, rows[3]).astype(jnp.bfloat16)
            kv = spheroid(cells, rows[4]).astype(jnp.bfloat16).astype(jnp.float32)
            proj = jnp.dot(tiles_t[label], ku, preferred_element_type=jnp.float32)
            model_re = jnp.sum(proj[:width] * kv, axis=0, keepdims=True)
            model_im = jnp.sum(proj[width:] * kv, axis=0, keepdims=True)
            res_re = rows[2] * (model_re - rows[0])
            res_im = rows[2] * (model_im - rows[1])
            residual[s, pl.ds(k, 1), :] = res_re
            residual[s, pl.ds(k + cap, 1), :] = res_im
            spread = jnp.concatenate(
                [(res_re * kv).astype(jnp.bfloat16), (res_im * kv).astype(jnp.bfloat16)], axis=0
            )
            contribs.append(
                lax.dot_general(
                    ku, spread, (((1,), (1,)), ((), ())), preferred_element_type=jnp.float32
                )
            )
        for g in range(group):
            label = labels[s * cap + k0 + g]
            gradient[label] = gradient[label] + contribs[g]
        return carry

    lax.fori_loop(0, came.shape[0] * per, body, 0)


def finish_kernel(
    n, m, cap, place, residual, gradient, grid, new_grid, res_out,
    back, part, own, send_sem, recv_sem, gsend_sem, grecv_sem, own_sem, mine_sem,
):
    me = lax.axis_index("bl")
    ch = lax.axis_index("chan")
    share = new_grid.shape[1]
    barrier = pltpu.get_barrier_semaphore()
    for d in range(1, m):
        pl.semaphore_signal(barrier, inc=1, device_id={"chan": lax.rem(ch + d, m)}, device_id_type=MESH)
    for d in range(1, n):
        pl.semaphore_signal(barrier, inc=1, device_id={"bl": lax.rem(me + d, n)}, device_id_type=MESH)
    pl.semaphore_wait(barrier, n - 1 + m - 1)
    sums = []
    for d in range(1, m):
        peer = lax.rem(ch + d, m)
        copy = pltpu.make_async_remote_copy(
            src_ref=gradient.at[:, pl.ds(pl.multiple_of(peer * share, share), share), :],
            dst_ref=part.at[d - 1],
            send_sem=gsend_sem.at[d],
            recv_sem=grecv_sem.at[d],
            device_id={"chan": peer},
            device_id_type=MESH,
        )
        copy.start()
        sums.append(copy)
    copies = []
    for d in range(1, n):
        peer = lax.rem(me + d, n)
        copy = pltpu.make_async_remote_copy(
            src_ref=residual.at[peer],
            dst_ref=back.at[pl.ds(pl.multiple_of(me * (2 * cap), 2 * cap), 2 * cap), :],
            send_sem=send_sem.at[d],
            recv_sem=recv_sem.at[d],
            device_id={"bl": peer},
            device_id_type=MESH,
        )
        copy.start()
        copies.append(copy)
    mine = pltpu.make_async_copy(
        residual.at[me], back.at[pl.ds(pl.multiple_of(me * (2 * cap), 2 * cap), 2 * cap), :], mine_sem
    )
    mine.start()
    first = pl.multiple_of(ch * share, share)
    held = pltpu.make_async_copy(grid.at[:, pl.ds(first, share), :], own, own_sem)
    held.start()
    mine.wait()
    for copy in copies:
        copy.wait()

    def unpack(b, carry):
        row = place[b]
        res_out[pl.ds(2 * b, 1), :] = back[pl.ds(row, 1), :]
        res_out[pl.ds(2 * b + 1, 1), :] = back[pl.ds(row + cap, 1), :]
        return carry

    lax.fori_loop(0, res_out.shape[0] // 2, unpack, 0, unroll=4)
    held.wait()
    total = gradient[:, pl.ds(first, share), :]
    for d, copy in enumerate(sums):
        copy.wait()
        total = total + part[d]
    base = own[...]
    new_grid[...] = base - step_length * (total + ridge_weight * base)


def shards(grid, tile_list, owner_map, offsets, positions, observed, weights):
    n = lax.axis_size("bl")
    m = lax.axis_size("chan")
    tile_dev, width, wide = grid.shape
    blocks, vis = tile_list.shape[1], positions.shape[3]
    cap = 2 * blocks // n
    lab_row = label_row(cap)
    f32 = jnp.float32
    out, place = pl.pallas_call(
        functools.partial(pack_kernel, cap, tile_dev),
        out_shape=(
            jax.ShapeDtypeStruct((n, lab_row + 8, vis), f32),
            jax.ShapeDtypeStruct((blocks,), jnp.int32),
        ),
        in_specs=[SMEM, SMEM, SMEM, VMEM, VMEM, VMEM],
        out_specs=(VMEM, SMEM),
        scratch_shapes=[pltpu.SMEM((n,), jnp.int32)],
        compiler_params=params(),
    )(
        tile_list,
        owner_map,
        offsets.reshape(2 * blocks),
        positions.reshape(2 * blocks, vis),
        observed.reshape(2 * blocks, vis),
        weights.reshape(blocks, vis),
    )
    dma = pltpu.SemaphoreType.DMA
    came, tiles_t = pl.pallas_call(
        functools.partial(exchange_kernel, n),
        out_shape=(
            jax.ShapeDtypeStruct(out.shape, f32),
            jax.ShapeDtypeStruct((tile_dev, wide, width), jnp.bfloat16),
        ),
        in_specs=[VMEM, VMEM],
        out_specs=(VMEM, VMEM),
        scratch_shapes=[dma((n,)), dma((n,)), dma],
        compiler_params=params(collective_id=0, has_side_effects=True),
    )(out, grid)
    labels = came[:, lab_row, :cap].astype(jnp.int32).reshape(n * cap)
    gradient, residual = pl.pallas_call(
        functools.partial(compute_kernel, cap, math.gcd(cap, 4)),
        out_shape=(
            jax.ShapeDtypeStruct(grid.shape, f32),
            jax.ShapeDtypeStruct((n, 2 * cap, vis), f32),
        ),
        in_specs=[SMEM, VMEM, VMEM],
        out_specs=(VMEM, VMEM),
        compiler_params=params(),
    )(labels, came, tiles_t)
    share = width // m
    new_grid, res_out = pl.pallas_call(
        functools.partial(finish_kernel, n, m, cap),
        out_shape=(
            jax.ShapeDtypeStruct((tile_dev, share, wide), f32),
            jax.ShapeDtypeStruct((2 * blocks, vis), f32),
        ),
        in_specs=[SMEM, VMEM, VMEM, ANY],
        out_specs=(VMEM, VMEM),
        scratch_shapes=[
            pltpu.VMEM((n * 2 * cap, vis), f32),
            pltpu.VMEM((m - 1, tile_dev, share, wide), f32),
            pltpu.VMEM((tile_dev, share, wide), f32),
            dma((n,)), dma((n,)), dma((m,)), dma((m,)), dma, dma,
        ],
        compiler_params=params(collective_id=1, has_side_effects=True),
    )(place, residual, gradient, grid)
    return (new_grid, res_out.reshape(1, blocks, 2, vis))


def solution(mesh):
    in_specs = (
        P("bl", None, None),
        P("chan", "bl"),
        P(),
        P("chan", "bl", None),
        P("chan", "bl", None, None),
        P("chan", "bl", None, None),
        P("chan", "bl", None),
    )
    out_specs = (P("bl", "chan", None), P("chan", "bl", None, None))
    return jax.shard_map(shards, mesh=mesh, in_specs=in_specs, out_specs=out_specs, check_vma=False)
```

time: 161 us -> 56.3 us (0.35)
  matrix products: 51.3 us -> 0 us
  Pallas kernels: 0 us -> 49.6 us
  waiting for transfers between devices: 36.6 us -> 0 us
  other arithmetic: 23.4 us -> 0.02 us
  starting transfers between devices: 14.8 us -> 0 us
  between operations: 14.1 us -> 0.71 us
  local copies, waits for them, and re-layouts: 18.7 us -> 5.69 us
    dot_general x24 -> x0, matrix products: 51.3 us -> none  [the longest x8 32.6 us: process(): jnp.einsum('gt,guw->tuw', selector, contrib, precision=lax.Precision.HIGH...]
    pallas_call x0 -> x4, Pallas kernels: none -> 49.6 us  [the longest x1 19.4 us: shards(): pl.pallas_call(functools.partial(finish_kernel, n, m, cap), out_shape=(ja...]
    all_to_all x3 -> x0, waiting for transfers between devices: 21.9 us -> none  [the longest x1 15.2 us: shards(): lax.all_to_all(outgoing, 'bl', split_axis=0, concat_axis=0, tiled=True)]
    all_to_all x3 -> x0, starting transfers between devices: 14.8 us -> none  [the longest x1 6.33 us: shards(): lax.all_to_all(slot_labels, 'bl', split_axis=0, concat_axis=0, tiled=True)]
    reduce_scatter x1 -> x0, waiting for transfers between devices: 14.7 us -> none  [shards(): lax.psum_scatter(gradient, 'chan', scatter_dimension=1, tiled=True)]
    reduce_sum x10 -> x0, other arithmetic: 10.5 us -> none  [the longest x8 9.41 us: degrid(): model_real = jnp.sum(projected[:, :, :tile_width] * kernel_wide, axis=2)]
    another operation x9 -> x0, other arithmetic: 8.17 us -> none
    scatter x2 -> x0, local copies, waits for them, and re-layouts: 7.23 us -> none  [the longest x1 6.46 us: shards(): jnp.zeros((slots_all,) + payload.shape[1:], jnp.float32).at[send_slot]]
  transfers between devices with their start and end apart: 4 -> 0, of which waited for: 3 -> 0; matrix products, arithmetic and copies ran while one was open for 8% -> 0% of each run, Pallas kernels for 0% -> 0%
where the time goes in v1:
time: 56.3 us; the launch traced here: 56 us
  Pallas kernels  49.6 us (88%)
  local copies, waits for them, and re-layouts  5.69 us (10%)
  between operations  0.71 us (1%)
    pallas_call x1, Pallas kernels, shards(): pl.pallas_call(functools.partial(finish_kernel, n, m, cap), out_shape=(ja...  19.4 us
    pallas_call x1, Pallas kernels, shards(): pl.pallas_call(functools.partial(compute_kernel, cap, math.gcd(cap, 4)),...  16.7 us
    pallas_call x1, Pallas kernels, shards(): pl.pallas_call(functools.partial(exchange_kernel, n), out_shape=(jax.Shap...  11.6 us
    unnamed x17, local copies, waits for them, and re-layouts  5.48 us
    pallas_call x1, Pallas kernels, shards(): pl.pallas_call(functools.partial(pack_kernel, cap, tile_dev), out_shape=(...  1.84 us

profile of v1, /device:TPU:0, one launch (start us, length us, event | category | flops | bytes accessed | tf_op | source)
XLA Modules:
  0.0 56.0 jit_solution(10590437495714568153)
XLA Ops:
  0.6 0.0 copy-start.2
  0.6 0.8 %copy.10 = s32[1,64,2]{2,1,0:T(8,128)S(1)} copy(s32[1,64,2]{1,2,0:T(2,128)} %param.10) | data formatting | bytes 1024 | tf_op args[3]
  1.4 0.0 copy-start.5
  1.4 0.0 copy-start.6
  1.5 0.1 reshape.22.offs
  1.6 0.0 copy-done.2
  1.6 0.5 copy-done.5
  2.1 0.0 copy-done.6
  2.1 0.0 copy-start.3
  2.1 0.8 %copy-done.3 = f32[1,64,2,128]{3,2,1,0:T(2,128)S(1)} copy-done((f32[1,64,2,128]{3,2,1,0:T(2,128)S(1)}, f32[1,64,2,128]{3,2,1,0:T(2,128)}, u32[]{:S(2)}) %copy-start.3) | copy-done | bytes 65560
  3.0 0.0 copy-start.4
  3.0 0.8 %copy-done.4 = f32[1,64,128]{2,1,0:T(8,128)S(1)} copy-done((f32[1,64,128]{2,1,0:T(8,128)S(1)}, f32[1,64,128]{2,1,0:T(8,128)}, u32[]{:S(2)}) %copy-start.4) | copy-done | bytes 32792
  3.7 1.8 %shard_map.86 = (f32[8,88,128]{2,1,0:T(8,128)S(1)}, s32[64]{0:T(128)S(1)}) custom-call(s32[1,64]{1,0:T(1,128)S(1)} %copy-done.5, s32[64]{0:T(128)S(1)} %copy-done.6, s32[128]{0:T(128)S(1)} %reshape.22.offs, f32[128,128]{1,0:T(8,128)S(1)} %bitcast.4, f32[128,128]{1,0:T(8,128)S(1)} %bitcast.5, f32[64,128]{1,0:T(8,128)S(1)} %bitcast.7), custom_call_target="tpu_custom_call" | custom-call | tf_op jit(solution)/shard_map/pallas_call | solution.py:211
  5.6 0.0 copy-start
  5.6 1.2 %copy-done = f32[8,128,256]{2,1,0:T(8,128)S(1)} copy-done((f32[8,128,256]{2,1,0:T(8,128)S(1)}, f32[8,128,256]{2,1,0:T(8,128)}, u32[]{:S(2)}) %copy-start) | copy-done | bytes 1048600
  6.8 0.0 copy-start.1
  6.8 11.6 %shard_map.87 = (f32[8,88,128]{2,1,0:T(8,128)S(1)}, bf16[8,256,128]{2,1,0:T(8,128)(2,1)S(1)}) custom-call(f32[8,88,128]{2,1,0:T(8,128)S(1)} %get-tuple-element.11.out, f32[8,128,256]{2,1,0:T(8,128)S(1)} %copy-done), custom_call_target="tpu_custom_call" | custom-call | tf_op jit(solution)/shard_map/pallas_call | solution.py:230
  18.4 0.1 convert_element_type.8.labels
  18.5 16.7 %shard_map.88 = (f32[8,128,256]{2,1,0:T(8,128)S(1)}, f32[8,32,128]{2,1,0:T(8,128)S(1)}) custom-call(s32[128]{0:T(128)S(1)} %convert_element_type.8.labels, f32[8,88,128]{2,1,0:T(8,128)S(1)} %get-tuple-element.12.came, bf16[8,256,128]{2,1,0:T(8,128)(2,1)S(1)} %get-tuple-element.13.tiles_t), custom_call_target="tpu_custom_call" | custom-call | tf_op jit(solution)/shard_map/pallas_call | solution.py:242
  35.2 0.0 copy-done.1
  35.2 19.4 %shard_map.89 = (f32[8,32,256]{2,1,0:T(8,128)S(1)}, f32[128,128]{1,0:T(8,128)S(1)}) custom-call(s32[64]{0:T(128)S(1)} %get-tuple-element.10.place, f32[8,32,128]{2,1,0:T(8,128)S(1)} %get-tuple-element.14.residual, f32[8,128,256]{2,1,0:T(8,128)S(1)} %get-tuple-element.15.gradient, f32[8,128,256]{2,1,0:T(8,128)S(1)} %copy-done.1), custom_call_target="tpu_custom_call" | custom-call | tf_op jit(solution)/shard_map/pallas_call | solution.py:253
  54.7 0.7 %copy.13 = f32[8,32,256]{2,1,0:T(8,128)} copy(f32[8,32,256]{2,1,0:T(8,128)S(1)} %get-tuple-element.20) | data formatting | bytes 524288
  55.4 0.6 %copy.14 = f32[1,64,2,128]{3,2,1,0:T(2,128)} copy(f32[1,64,2,128]{3,2,1,0:T(2,128)S(1)} %bitcast.6) | data formatting | bytes 131072
  (1 shorter events, 0.0 us)
Async XLA Ops:
  0.6 1.0 %copy-start.2 = (f32[1,64,2,128]{3,2,1,0:T(2,128)S(1)}, f32[1,64,2,128]{3,2,1,0:T(2,128)}, u32[]{:S(2)}) copy-start(f32[1,64,2,128]{3,2,1,0:T(2,128)} %param.11) | copy-start | bytes 196612
  1.4 0.7 %copy-start.5 = (s32[1,64]{1,0:T(1,128)S(1)}, s32[1,64]{1,0:T(1,128)}, u32[]{:S(2)}) copy-start(s32[1,64]{1,0:T(1,128)} %tiles.1) | copy-start | bytes 772
  1.4 0.7 %copy-start.6 = (s32[64]{0:T(128)S(1)}, s32[64]{0:T(128)}, u32[]{:S(2)}) copy-start(s32[64]{0:T(128)} %owners.1) | copy-start | bytes 772
  2.1 0.8 %copy-start.3 = (f32[1,64,2,128]{3,2,1,0:T(2,128)S(1)}, f32[1,64,2,128]{3,2,1,0:T(2,128)}, u32[]{:S(2)}) copy-start(f32[1,64,2,128]{3,2,1,0:T(2,128)} %param.12) | copy-start | bytes 196612
  3.0 0.8 %copy-start.4 = (f32[1,64,128]{2,1,0:T(8,128)S(1)}, f32[1,64,128]{2,1,0:T(8,128)}, u32[]{:S(2)}) copy-start(f32[1,64,128]{2,1,0:T(8,128)} %param.13) | copy-start | bytes 98308
  5.6 1.2 %copy-start = (f32[8,128,256]{2,1,0:T(8,128)S(1)}, f32[8,128,256]{2,1,0:T(8,128)}, u32[]{:S(2)}) copy-start(f32[8,128,256]{2,1,0:T(8,128)} %grid.3) | copy-start | bytes 3145732
  6.8 28.4 %copy-start.1 = (f32[8,128,256]{2,1,0:T(8,128)S(1)}, f32[8,128,256]{2,1,0:T(8,128)}, u32[]{:S(2)}) copy-start(f32[8,128,256]{2,1,0:T(8,128)} %grid.3) | copy-start | bytes 3145732

commit v2 on v1

v2 whole, which is shorter than its diff:
```python
import functools
import math

import jax
import jax.numpy as jnp
from jax import lax
from jax.experimental import pallas as pl
from jax.experimental.pallas import tpu as pltpu
from jax.sharding import PartitionSpec as P

kernel_beta = 18.4
half_support = 4.0
step_length = 1.0
ridge_weight = 0.5
exponent_scale = kernel_beta / math.log(2.0)
MESH = pl.DeviceIdType.MESH
VMEM = pl.BlockSpec(memory_space=pltpu.VMEM)
SMEM = pl.BlockSpec(memory_space=pltpu.SMEM)
ANY = pl.BlockSpec(memory_space=pltpu.HBM)


def params(limit=24, **kw):
    return pltpu.CompilerParams(vmem_limit_bytes=limit * 2**20, **kw)


def pad_rows(cap):
    return -(-5 * cap // 8) * 8


def pack_kernel(
    cap, tile_dev, tiles, owners, offs, pos_in, obs_in, wts_in, out, labels, place,
    count, pos, obs, wts, sems,
):
    loads = [
        pltpu.make_async_copy(src, dst, sems.at[i])
        for i, (src, dst) in enumerate(((pos_in, pos), (obs_in, obs), (wts_in, wts)))
    ]
    for load in loads:
        load.start()
    blocks = wts.shape[0]
    out[...] = jnp.zeros_like(out)
    labels[...] = jnp.zeros_like(labels)
    for o in range(out.shape[0]):
        count[o] = 0
    lane = lax.broadcasted_iota(jnp.int32, (1, out.shape[2]), 1)
    for load in loads:
        load.wait()

    def body(b, carry):
        slot = owners[tiles[0, b]]
        o = lax.div(slot, tile_dev)
        local = lax.rem(slot, tile_dev)
        r = count[o]
        count[o] = r + 1
        place[b] = o * (2 * cap) + r
        out[o, pl.ds(r, 1), :] = obs[pl.ds(2 * b, 1), :]
        out[o, pl.ds(r + cap, 1), :] = obs[pl.ds(2 * b + 1, 1), :]
        out[o, pl.ds(r + 2 * cap, 1), :] = wts[pl.ds(b, 1), :]
        u_shift = offs[0, b].astype(jnp.float32)
        v_shift = offs[1, b].astype(jnp.float32)
        out[o, pl.ds(r + 3 * cap, 1), :] = u_shift + pos[pl.ds(2 * b, 1), :]
        out[o, pl.ds(r + 4 * cap, 1), :] = v_shift + pos[pl.ds(2 * b + 1, 1), :]
        old = labels[o, pl.ds(0, 1), :]
        labels[o, pl.ds(0, 1), :] = jnp.where(lane == r, local, old)
        return carry

    lax.fori_loop(0, blocks, body, 0, unroll=4)


def spheroid(cells, coord):
    d = cells - coord * (1.0 / half_support)
    y = 1.0 - d * d
    ym = jnp.maximum(y, 1e-30)
    z = ym * lax.rsqrt(ym) * exponent_scale - exponent_scale
    return jnp.where(y > 0.0, jnp.exp2(z), 0.0)


def partner(me, d, n):
    peer, bit = me, 1
    while bit < n:
        has = lax.rem(lax.div(d, bit), 2) if not isinstance(d, int) else (d // bit) % 2
        peer = peer + has * bit * (1 - 2 * lax.rem(lax.div(me, bit), 2))
        bit *= 2
    return peer


def degrid_kernel(
    n, cap, group, out, labels, grid_in, came_lab, ku_all, spread_all, residual,
    grid, tiles_t, came, lab_s, send_sem, recv_sem, lsend_sem, lrecv_sem, grid_sem, own_sem, smem_sem,
):
    load = pltpu.make_async_copy(grid_in, grid, grid_sem)
    load.start()
    me = lax.axis_index("bl")
    barrier = pltpu.get_barrier_semaphore()
    for d in range(1, n):
        pl.semaphore_signal(barrier, inc=1, device_id={"bl": partner(me, d, n)}, device_id_type=MESH)
    own_lab = pltpu.make_async_copy(labels.at[me], came_lab.at[me], own_sem.at[0])
    own_lab.start()
    own = pltpu.make_async_copy(out.at[me], came.at[me], own_sem.at[1])
    own.start()
    pl.semaphore_wait(barrier, n - 1)

    def label_copy(d):
        peer = partner(me, d, n)
        return pltpu.make_async_remote_copy(
            src_ref=labels.at[peer],
            dst_ref=came_lab.at[me],
            send_sem=lsend_sem.at[d],
            recv_sem=lrecv_sem.at[d],
            device_id={"bl": peer},
            device_id_type=MESH,
        )

    def data_copy(d):
        peer = partner(me, d, n)
        return pltpu.make_async_remote_copy(
            src_ref=out.at[peer],
            dst_ref=came.at[me],
            send_sem=send_sem.at[d],
            recv_sem=recv_sem.at[d],
            device_id={"bl": peer},
            device_id_type=MESH,
        )

    for d in range(1, n):
        label_copy(d).start()
    for d in range(1, n):
        data_copy(d).start()
    load.wait()
    for t in range(grid.shape[0]):
        tiles_t[t] = grid[t].T.astype(jnp.bfloat16)
    own_lab.wait()
    for d in range(1, n):
        label_copy(d).wait()
    to_smem = pltpu.make_async_copy(came_lab, lab_s, smem_sem)
    to_smem.start()
    to_smem.wait()
    width = tiles_t.shape[2]
    vis = came.shape[2]

    def chunk(s):
        def body(i, carry):
            k0 = i * group
            cells = lax.broadcasted_iota(jnp.int32, (width, vis), 0).astype(jnp.float32) * (
                1.0 / half_support
            )
            for g in range(group):
                k = k0 + g
                label = lab_s[s, 0, k]
                rows = [came[s, pl.ds(k + c * cap, 1), :] for c in range(5)]
                ku = spheroid(cells, rows[3]).astype(jnp.bfloat16)
                kv = spheroid(cells, rows[4]).astype(jnp.bfloat16).astype(jnp.float32)
                proj = jnp.dot(tiles_t[label], ku, preferred_element_type=jnp.float32)
                model_re = jnp.sum(proj[:width] * kv, axis=0, keepdims=True)
                model_im = jnp.sum(proj[width:] * kv, axis=0, keepdims=True)
                res_re = rows[2] * (model_re - rows[0])
                res_im = rows[2] * (model_im - rows[1])
                residual[s, pl.ds(k, 1), :] = res_re
                residual[s, pl.ds(k + cap, 1), :] = res_im
                at = s * cap + k
                ku_all[at] = ku
                spread_all[at, :width, :] = (res_re * kv).astype(jnp.bfloat16)
                spread_all[at, width:, :] = (res_im * kv).astype(jnp.bfloat16)
            return carry

        lax.fori_loop(0, cap // group, body, 0)

    own.wait()
    chunk(me)

    def arrived(d, carry):
        data_copy(d).wait_recv()
        chunk(partner(me, d, n))
        return carry

    lax.fori_loop(1, n, arrived, 0)
    for d in range(1, n):
        data_copy(d).wait_send()


def gradient_kernel(cap, group, labels, ku_all, spread_all, gradient):
    gradient[...] = jnp.zeros_like(gradient)
    per = cap // group

    def body(i, carry):
        s = lax.div(i, per)
        k0 = lax.rem(i, per) * group
        contribs = [
            lax.dot_general(
                ku_all[i * group + g],
                spread_all[i * group + g],
                (((1,), (1,)), ((), ())),
                preferred_element_type=jnp.float32,
            )
            for g in range(group)
        ]
        for g in range(group):
            label = labels[s, 0, k0 + g]
            gradient[label] = gradient[label] + contribs[g]
        return carry

    lax.fori_loop(0, labels.shape[0] * per, body, 0)


def finish_kernel(
    n, m, cap, place, residual, gradient, grid, new_grid, res_out,
    back, part, own, send_sem, recv_sem, gsend_sem, grecv_sem, own_sem, mine_sem,
):
    me = lax.axis_index("bl")
    ch = lax.axis_index("chan")
    share = new_grid.shape[1]
    barrier = pltpu.get_barrier_semaphore()
    for d in range(1, m):
        pl.semaphore_signal(barrier, inc=1, device_id={"chan": lax.rem(ch + d, m)}, device_id_type=MESH)
    for d in range(1, n):
        pl.semaphore_signal(barrier, inc=1, device_id={"bl": lax.rem(me + d, n)}, device_id_type=MESH)
    pl.semaphore_wait(barrier, n - 1 + m - 1)
    sums = []
    for d in range(1, m):
        peer = lax.rem(ch + d, m)
        copy = pltpu.make_async_remote_copy(
            src_ref=gradient.at[:, pl.ds(pl.multiple_of(peer * share, share), share), :],
            dst_ref=part.at[d - 1],
            send_sem=gsend_sem.at[d],
            recv_sem=grecv_sem.at[d],
            device_id={"chan": peer},
            device_id_type=MESH,
        )
        copy.start()
        sums.append(copy)
    copies = []
    for d in range(1, n):
        peer = lax.rem(me + d, n)
        copy = pltpu.make_async_remote_copy(
            src_ref=residual.at[peer],
            dst_ref=back.at[pl.ds(pl.multiple_of(me * (2 * cap), 2 * cap), 2 * cap), :],
            send_sem=send_sem.at[d],
            recv_sem=recv_sem.at[d],
            device_id={"bl": peer},
            device_id_type=MESH,
        )
        copy.start()
        copies.append(copy)
    mine = pltpu.make_async_copy(
        residual.at[me], back.at[pl.ds(pl.multiple_of(me * (2 * cap), 2 * cap), 2 * cap), :], mine_sem
    )
    mine.start()
    first = pl.multiple_of(ch * share, share)
    held = pltpu.make_async_copy(grid.at[:, pl.ds(first, share), :], own, own_sem)
    held.start()
    mine.wait()
    for copy in copies:
        copy.wait()

    def unpack(b, carry):
        row = place[b]
        res_out[pl.ds(2 * b, 1), :] = back[pl.ds(row, 1), :]
        res_out[pl.ds(2 * b + 1, 1), :] = back[pl.ds(row + cap, 1), :]
        return carry

    lax.fori_loop(0, res_out.shape[0] // 2, unpack, 0, unroll=4)
    held.wait()
    total = gradient[:, pl.ds(first, share), :]
    for d, copy in enumerate(sums):
        copy.wait()
        total = total + part[d]
    base = own[...]
    new_grid[...] = base - step_length * (total + ridge_weight * base)


def shards(grid, tile_list, owner_map, offsets, positions, observed, weights):
    n = lax.axis_size("bl")
    m = lax.axis_size("chan")
    tile_dev, width, wide = grid.shape
    blocks, vis = tile_list.shape[1], positions.shape[3]
    cap = 2 * blocks // n
    f32 = jnp.float32
    dma = pltpu.SemaphoreType.DMA
    out, labels, place = pl.pallas_call(
        functools.partial(pack_kernel, cap, tile_dev),
        out_shape=(
            jax.ShapeDtypeStruct((n, pad_rows(cap), vis), f32),
            jax.ShapeDtypeStruct((n, 8, vis), jnp.int32),
            jax.ShapeDtypeStruct((blocks,), jnp.int32),
        ),
        in_specs=[SMEM, SMEM, SMEM, ANY, ANY, ANY],
        out_specs=(VMEM, VMEM, SMEM),
        scratch_shapes=[
            pltpu.SMEM((n,), jnp.int32),
            pltpu.VMEM((2 * blocks, vis), f32),
            pltpu.VMEM((2 * blocks, vis), f32),
            pltpu.VMEM((blocks, vis), f32),
            dma((3,)),
        ],
        compiler_params=params(60),
    )(
        tile_list,
        owner_map,
        jnp.swapaxes(offsets[0], 0, 1),
        positions.reshape(2 * blocks, vis),
        observed.reshape(2 * blocks, vis),
        weights.reshape(blocks, vis),
    )
    group = math.gcd(cap, 4)
    came_lab, ku_all, spread_all, residual = pl.pallas_call(
        functools.partial(degrid_kernel, n, cap, group),
        out_shape=(
            jax.ShapeDtypeStruct((n, 8, vis), jnp.int32),
            jax.ShapeDtypeStruct((n * cap, width, vis), jnp.bfloat16),
            jax.ShapeDtypeStruct((n * cap, wide, vis), jnp.bfloat16),
            jax.ShapeDtypeStruct((n, 2 * cap, vis), f32),
        ),
        in_specs=[VMEM, VMEM, ANY],
        out_specs=(VMEM, VMEM, VMEM, VMEM),
        scratch_shapes=[
            pltpu.VMEM(grid.shape, f32),
            pltpu.VMEM((tile_dev, wide, width), jnp.bfloat16),
            pltpu.VMEM(out.shape, f32),
            pltpu.SMEM((n, 8, vis), jnp.int32),
            dma((n,)), dma((n,)), dma((n,)), dma((n,)), dma, dma((2,)), dma,
        ],
        compiler_params=params(collective_id=0, has_side_effects=True),
    )(out, labels, grid)
    gradient = pl.pallas_call(
        functools.partial(gradient_kernel, cap, group),
        out_shape=jax.ShapeDtypeStruct(grid.shape, f32),
        in_specs=[SMEM, VMEM, VMEM],
        out_specs=VMEM,
        compiler_params=params(),
    )(came_lab, ku_all, spread_all)
    share = width // m
    new_grid, res_out = pl.pallas_call(
        functools.partial(finish_kernel, n, m, cap),
        out_shape=(
            jax.ShapeDtypeStruct((tile_dev, share, wide), f32),
            jax.ShapeDtypeStruct((2 * blocks, vis), f32),
        ),
        in_specs=[SMEM, VMEM, VMEM, ANY],
        out_specs=(VMEM, VMEM),
        scratch_shapes=[
            pltpu.VMEM((n * 2 * cap, vis), f32),
            pltpu.VMEM((m - 1, tile_dev, share, wide), f32),
            pltpu.VMEM((tile_dev, share, wide), f32),
            dma((n,)), dma((n,)), dma((m,)), dma((m,)), dma, dma,
        ],
        compiler_params=params(collective_id=1, has_side_effects=True),
    )(place, residual, gradient, grid)
    return (new_grid, res_out.reshape(1, blocks, 2, vis))


def solution(mesh):
    in_specs = (
        P("bl", None, None),
        P("chan", "bl"),
        P(),
        P("chan", "bl", None),
        P("chan", "bl", None, None),
        P("chan", "bl", None, None),
        P("chan", "bl", None),
    )
    out_specs = (P("bl", "chan", None), P("chan", "bl", None, None))
    return jax.shard_map(shards, mesh=mesh, in_specs=in_specs, out_specs=out_specs, check_vma=False)
```

time: 56.3 us -> 55.7 us (0.989)
  local copies, waits for them, and re-layouts: 5.69 us -> 4.3 us
  Pallas kernels: 49.6 us -> 50.4 us
    pallas_call x1, Pallas kernels: 19.4 us -> 18 us  [shards(): pl.pallas_call(functools.partial(finish_kernel, n, m, cap), out_shape=(ja...]
    pallas_call x1, Pallas kernels: 1.84 us -> 3.03 us  [shards(): pl.pallas_call(functools.partial(pack_kernel, cap, tile_dev), out_shape=(...]
    unnamed x17 -> x12, local copies, waits for them, and re-layouts: 5.48 us -> 4.3 us
    pallas_call x2, Pallas kernels: 28.3 us -> 29.4 us  [the longest x1 20.5 us: shards(): pl.pallas_call(functools.partial(degrid_kernel, n, cap, group), out_shape...]
where the time goes in v2:
time: 55.7 us; the launch traced here: 55.4 us
  Pallas kernels  50.4 us (90%)
  local copies, waits for them, and re-layouts  4.3 us (8%)
  between operations  0.7 us (1%)
    pallas_call x1, Pallas kernels, shards(): pl.pallas_call(functools.partial(degrid_kernel, n, cap, group), out_shape...  20.5 us
    pallas_call x1, Pallas kernels, shards(): pl.pallas_call(functools.partial(finish_kernel, n, m, cap), out_shape=(ja...  18 us
    pallas_call x1, Pallas kernels, shards(): pl.pallas_call(functools.partial(gradient_kernel, cap, group), out_shape=...  8.88 us
    unnamed x12, local copies, waits for them, and re-layouts  4.3 us
    pallas_call x1, Pallas kernels, shards(): pl.pallas_call(functools.partial(pack_kernel, cap, tile_dev), out_shape=(...  3.03 us

profile of v2, /device:TPU:0, one launch (start us, length us, event | category | flops | bytes accessed | tf_op | source)
XLA Modules:
  0.0 55.4 jit_solution(9189244143739681306)
XLA Ops:
  0.6 3.0 %shard_map.86 = (f32[8,80,128]{2,1,0:T(8,128)}, s32[8,8,128]{2,1,0:T(8,128)}, s32[64]{0:T(128)}) custom-call(s32[1,64]{1,0:T(1,128)} %tiles.1, s32[64]{0:T(128)} %owners.1, s32[2,64]{1,0:T(2,128)} %bitcast.11, f32[128,128]{1,0:T(8,128)} %bitcast.8, f32[128,128]{1,0:T(8,128)} %bitcast.9, f32[64,128]{1,0:T(8,128)} %bitcast.10), custom_call_target="tpu_custom_call" | custom-call | tf_op jit(solution)/shard_map/pallas_call | solution.py:279
  3.7 0.0 copy-start.4
  3.7 0.0 copy-start
  3.7 1.2 %copy-done = f32[8,128,256]{2,1,0:T(8,128)S(1)} copy-done((f32[8,128,256]{2,1,0:T(8,128)S(1)}, f32[8,128,256]{2,1,0:T(8,128)}, u32[]{:S(2)}) %copy-start) | copy-done | bytes 1048600
  4.9 0.0 copy-start.2
  4.9 1.0 %copy-done.2 = f32[8,80,128]{2,1,0:T(8,128)S(1)} copy-done((f32[8,80,128]{2,1,0:T(8,128)S(1)}, f32[8,80,128]{2,1,0:T(8,128)}, u32[]{:S(2)}) %copy-start.2) | copy-done | bytes 327704
  5.9 0.0 copy-start.3
  5.9 0.8 %copy-done.3 = s32[8,8,128]{2,1,0:T(8,128)S(1)} copy-done((s32[8,8,128]{2,1,0:T(8,128)S(1)}, s32[8,8,128]{2,1,0:T(8,128)}, u32[]{:S(2)}) %copy-start.3) | copy-done | bytes 32792
  6.6 0.0 copy-start.1
  6.6 20.5 %shard_map.87 = (s32[8,8,128]{2,1,0:T(8,128)S(1)}, bf16[128,128,128]{2,1,0:T(8,128)(2,1)S(1)}, bf16[128,256,128]{2,1,0:T(8,128)(2,1)S(1)}, f32[8,32,128]{2,1,0:T(8,128)S(1)}) custom-call(f32[8,80,128]{2,1,0:T(8,128)S(1)} %copy-done.2, s32[8,8,128]{2,1,0:T(8,128)S(1)} %copy-done.3, f32[8,128,256]{2,1,0:T(8,128)S(1)} %copy-done), custom_call_target="tpu_custom_call" | custom-call | tf_op jit(solution)/shard_map/pallas_call | solution.py:305
  27.2 8.9 %shard_map.88.gradient = f32[8,128,256]{2,1,0:T(8,128)S(1)} custom-call(s32[8,8,128]{2,1,0:T(8,128)S(1)} %get-tuple-element.15.labels, bf16[128,128,128]{2,1,0:T(8,128)(2,1)S(1)} %get-tuple-element.16.ku_all, bf16[128,256,128]{2,1,0:T(8,128)(2,1)S(1)} %get-tuple-element.17.spread_all), custom_call_target="tpu_custom_call" | custom-call | tf_op jit(solution)/shard_map/pallas_call | solution.py:324
  36.0 0.0 copy-done.4
  36.1 0.0 copy-done.1
  36.1 18.0 %shard_map.89 = (f32[8,32,256]{2,1,0:T(8,128)S(1)}, f32[128,128]{1,0:T(8,128)S(1)}) custom-call(s32[64]{0:T(128)S(1)} %copy-done.4, f32[8,32,128]{2,1,0:T(8,128)S(1)} %get-tuple-element.14.residual, f32[8,128,256]{2,1,0:T(8,128)S(1)} %shard_map.88.gradient, f32[8,128,256]{2,1,0:T(8,128)S(1)} %copy-done.1), custom_call_target="tpu_custom_call" | custom-call | tf_op jit(solution)/shard_map/pallas_call | solution.py:332
  54.1 0.7 %copy.11 = f32[8,32,256]{2,1,0:T(8,128)} copy(f32[8,32,256]{2,1,0:T(8,128)S(1)} %get-tuple-element.22) | data formatting | bytes 524288
  54.8 0.6 %copy.12 = f32[1,64,2,128]{3,2,1,0:T(2,128)} copy(f32[1,64,2,128]{3,2,1,0:T(2,128)S(1)} %bitcast.7) | data formatting | bytes 131072
Async XLA Ops:
  3.7 32.4 %copy-start.4 = (s32[64]{0:T(128)S(1)}, s32[64]{0:T(128)}, u32[]{:S(2)}) copy-start(s32[64]{0:T(128)} %get-tuple-element.11.place) | copy-start | bytes 772
  3.7 1.2 %copy-start = (f32[8,128,256]{2,1,0:T(8,128)S(1)}, f32[8,128,256]{2,1,0:T(8,128)}, u32[]{:S(2)}) copy-start(f32[8,128,256]{2,1,0:T(8,128)} %grid.1) | copy-start | bytes 3145732
  4.9 1.0 %copy-start.2 = (f32[8,80,128]{2,1,0:T(8,128)S(1)}, f32[8,80,128]{2,1,0:T(8,128)}, u32[]{:S(2)}) copy-start(f32[8,80,128]{2,1,0:T(8,128)} %get-tuple-element.12.out) | copy-start | bytes 983044
  5.9 0.8 %copy-start.3 = (s32[8,8,128]{2,1,0:T(8,128)S(1)}, s32[8,8,128]{2,1,0:T(8,128)}, u32[]{:S(2)}) copy-start(s32[8,8,128]{2,1,0:T(8,128)} %get-tuple-element.13.labels) | copy-start | bytes 98308
  6.6 29.4 %copy-start.1 = (f32[8,128,256]{2,1,0:T(8,128)S(1)}, f32[8,128,256]{2,1,0:T(8,128)}, u32[]{:S(2)}) copy-start(f32[8,128,256]{2,1,0:T(8,128)} %grid.1) | copy-start | bytes 3145732

commit v3 on v2

--- a/solution.py
+++ b/solution.py
@@ -144,23 +144,29 @@
             cells = lax.broadcasted_iota(jnp.int32, (width, vis), 0).astype(jnp.float32) * (
                 1.0 / half_support
             )
-            for g in range(group):
-                k = k0 + g
-                label = lab_s[s, 0, k]
-                rows = [came[s, pl.ds(k + c * cap, 1), :] for c in range(5)]
-                ku = spheroid(cells, rows[3]).astype(jnp.bfloat16)
-                kv = spheroid(cells, rows[4]).astype(jnp.bfloat16).astype(jnp.float32)
-                proj = jnp.dot(tiles_t[label], ku, preferred_element_type=jnp.float32)
-                model_re = jnp.sum(proj[:width] * kv, axis=0, keepdims=True)
-                model_im = jnp.sum(proj[width:] * kv, axis=0, keepdims=True)
-                res_re = rows[2] * (model_re - rows[0])
-                res_im = rows[2] * (model_im - rows[1])
-                residual[s, pl.ds(k, 1), :] = res_re
-                residual[s, pl.ds(k + cap, 1), :] = res_im
-                at = s * cap + k
-                ku_all[at] = ku
-                spread_all[at, :width, :] = (res_re * kv).astype(jnp.bfloat16)
-                spread_all[at, width:, :] = (res_im * kv).astype(jnp.bfloat16)
+            each = range(group)
+            rows = [[came[s, pl.ds(k0 + g + c * cap, 1), :] for c in range(5)] for g in each]
+            held = [tiles_t[lab_s[s, 0, k0 + g]] for g in each]
+            kus = [spheroid(cells, rows[g][3]).astype(jnp.bfloat16) for g in each]
+            projs = [jnp.dot(held[g], kus[g], preferred_element_type=jnp.float32) for g in each]
+            kvs = [
+                spheroid(cells, rows[g][4]).astype(jnp.bfloat16).astype(jnp.float32) for g in each
+            ]
+            res_re = [
+                rows[g][2] * (jnp.sum(projs[g][:width] * kvs[g], axis=0, keepdims=True) - rows[g][0])
+                for g in each
+            ]
+            res_im = [
+                rows[g][2] * (jnp.sum(projs[g][width:] * kvs[g], axis=0, keepdims=True) - rows[g][1])
+                for g in each
+            ]
+            for g in each:
+                at = s * cap + k0 + g
+                residual[s, pl.ds(k0 + g, 1), :] = res_re[g]
+                residual[s, pl.ds(k0 + g + cap, 1), :] = res_im[g]
+                ku_all[at] = kus[g]
+                spread_all[at, :width, :] = (res_re[g] * kvs[g]).astype(jnp.bfloat16)
+                spread_all[at, width:, :] = (res_im[g] * kvs[g]).astype(jnp.bfloat16)
             return carry
 
         lax.fori_loop(0, cap // group, body, 0)

time: 55.7 us -> 55.7 us (level)
  no operation moved by 1% of the time
where the time goes in v3:
time: 55.7 us; the launch traced here: 55.4 us
  Pallas kernels  50.4 us (90%)
  local copies, waits for them, and re-layouts  4.3 us (8%)
  between operations  0.7 us (1%)
    pallas_call x1, Pallas kernels, shards(): pl.pallas_call(functools.partial(degrid_kernel, n, cap, group), out_shape...  20.5 us
    pallas_call x1, Pallas kernels, shards(): pl.pallas_call(functools.partial(finish_kernel, n, m, cap), out_shape=(ja...  18 us
    pallas_call x1, Pallas kernels, shards(): pl.pallas_call(functools.partial(gradient_kernel, cap, group), out_shape=...  8.89 us
    unnamed x12, local copies, waits for them, and re-layouts  4.3 us
    pallas_call x1, Pallas kernels, shards(): pl.pallas_call(functools.partial(pack_kernel, cap, tile_dev), out_shape=(...  3.03 us

profile of v3, /device:TPU:0, one launch (start us, length us, event | category | flops | bytes accessed | tf_op | source)
XLA Modules:
  0.0 55.4 jit_solution(12103442501270642493)
XLA Ops:
  0.6 3.0 %shard_map.86 = (f32[8,80,128]{2,1,0:T(8,128)}, s32[8,8,128]{2,1,0:T(8,128)}, s32[64]{0:T(128)}) custom-call(s32[1,64]{1,0:T(1,128)} %tiles.1, s32[64]{0:T(128)} %owners.1, s32[2,64]{1,0:T(2,128)} %bitcast.11, f32[128,128]{1,0:T(8,128)} %bitcast.8, f32[128,128]{1,0:T(8,128)} %bitcast.9, f32[64,128]{1,0:T(8,128)} %bitcast.10), custom_call_target="tpu_custom_call" | custom-call | tf_op jit(solution)/shard_map/pallas_call | solution.py:285
  3.7 0.0 copy-start.4
  3.7 0.0 copy-start
  3.7 1.2 %copy-done = f32[8,128,256]{2,1,0:T(8,128)S(1)} copy-done((f32[8,128,256]{2,1,0:T(8,128)S(1)}, f32[8,128,256]{2,1,0:T(8,128)}, u32[]{:S(2)}) %copy-start) | copy-done | bytes 1048600
  4.9 0.0 copy-start.2
  4.9 1.0 %copy-done.2 = f32[8,80,128]{2,1,0:T(8,128)S(1)} copy-done((f32[8,80,128]{2,1,0:T(8,128)S(1)}, f32[8,80,128]{2,1,0:T(8,128)}, u32[]{:S(2)}) %copy-start.2) | copy-done | bytes 327704
  5.9 0.0 copy-start.3
  5.9 0.8 %copy-done.3 = s32[8,8,128]{2,1,0:T(8,128)S(1)} copy-done((s32[8,8,128]{2,1,0:T(8,128)S(1)}, s32[8,8,128]{2,1,0:T(8,128)}, u32[]{:S(2)}) %copy-start.3) | copy-done | bytes 32792
  6.6 0.0 copy-start.1
  6.6 20.5 %shard_map.87 = (s32[8,8,128]{2,1,0:T(8,128)S(1)}, bf16[128,128,128]{2,1,0:T(8,128)(2,1)S(1)}, bf16[128,256,128]{2,1,0:T(8,128)(2,1)S(1)}, f32[8,32,128]{2,1,0:T(8,128)S(1)}) custom-call(f32[8,80,128]{2,1,0:T(8,128)S(1)} %copy-done.2, s32[8,8,128]{2,1,0:T(8,128)S(1)} %copy-done.3, f32[8,128,256]{2,1,0:T(8,128)S(1)} %copy-done), custom_call_target="tpu_custom_call" | custom-call | tf_op jit(solution)/shard_map/pallas_call | solution.py:311
  27.2 8.9 %shard_map.88.gradient = f32[8,128,256]{2,1,0:T(8,128)S(1)} custom-call(s32[8,8,128]{2,1,0:T(8,128)S(1)} %get-tuple-element.15.labels, bf16[128,128,128]{2,1,0:T(8,128)(2,1)S(1)} %get-tuple-element.16.ku_all, bf16[128,256,128]{2,1,0:T(8,128)(2,1)S(1)} %get-tuple-element.17.spread_all), custom_call_target="tpu_custom_call" | custom-call | tf_op jit(solution)/shard_map/pallas_call | solution.py:330
  36.1 0.0 copy-done.4
  36.1 0.0 copy-done.1
  36.1 18.0 %shard_map.89 = (f32[8,32,256]{2,1,0:T(8,128)S(1)}, f32[128,128]{1,0:T(8,128)S(1)}) custom-call(s32[64]{0:T(128)S(1)} %copy-done.4, f32[8,32,128]{2,1,0:T(8,128)S(1)} %get-tuple-element.14.residual, f32[8,128,256]{2,1,0:T(8,128)S(1)} %shard_map.88.gradient, f32[8,128,256]{2,1,0:T(8,128)S(1)} %copy-done.1), custom_call_target="tpu_custom_call" | custom-call | tf_op jit(solution)/shard_map/pallas_call | solution.py:338
  54.1 0.7 %copy.11 = f32[8,32,256]{2,1,0:T(8,128)} copy(f32[8,32,256]{2,1,0:T(8,128)S(1)} %get-tuple-element.22) | data formatting | bytes 524288
  54.8 0.6 %copy.12 = f32[1,64,2,128]{3,2,1,0:T(2,128)} copy(f32[1,64,2,128]{3,2,1,0:T(2,128)S(1)} %bitcast.7) | data formatting | bytes 131072
Async XLA Ops:
  3.7 32.4 %copy-start.4 = (s32[64]{0:T(128)S(1)}, s32[64]{0:T(128)}, u32[]{:S(2)}) copy-start(s32[64]{0:T(128)} %get-tuple-element.11.place) | copy-start | bytes 772
  3.7 1.2 %copy-start = (f32[8,128,256]{2,1,0:T(8,128)S(1)}, f32[8,128,256]{2,1,0:T(8,128)}, u32[]{:S(2)}) copy-start(f32[8,128,256]{2,1,0:T(8,128)} %grid.1) | copy-start | bytes 3145732
  4.9 1.0 %copy-start.2 = (f32[8,80,128]{2,1,0:T(8,128)S(1)}, f32[8,80,128]{2,1,0:T(8,128)}, u32[]{:S(2)}) copy-start(f32[8,80,128]{2,1,0:T(8,128)} %get-tuple-element.12.out) | copy-start | bytes 983044
  5.9 0.8 %copy-start.3 = (s32[8,8,128]{2,1,0:T(8,128)S(1)}, s32[8,8,128]{2,1,0:T(8,128)}, u32[]{:S(2)}) copy-start(s32[8,8,128]{2,1,0:T(8,128)} %get-tuple-element.13.labels) | copy-start | bytes 98308
  6.6 29.4 %copy-start.1 = (f32[8,128,256]{2,1,0:T(8,128)S(1)}, f32[8,128,256]{2,1,0:T(8,128)}, u32[]{:S(2)}) copy-start(f32[8,128,256]{2,1,0:T(8,128)} %grid.1) | copy-start | bytes 3145732
